TPU v7x, 32 devices: a whole 2x2x4 slice. The times are simulated.
32 devices in a mesh: batch: 4 (over x, core), ctx: 8 (over z, y).
Axes of the slice: x: 2, y: 2, z: 4, core: 2. Of those that a mesh axis runs over, the one named last changes fastest.
Arguments:
- event_rows: bfloat16 [4, 2048, 256], P('batch', 'ctx'), may hold values from -6 to 6
- event_index: int32 [4, 2048], P('batch', 'ctx'), may hold values from 0 to 16383, as said below
- decay: float32 [4, 16, 2048], P('batch', None, 'ctx'), may hold values from 0.15 to 1
- saved_state: float32 [4, 8, 16, 128, 64], P('batch', 'ctx'), may hold values from -6 to 6
- dout: bfloat16 [4, 2048, 512], P('batch', 'ctx'), may hold values from -0.29882812 to 0.29882812
- w_up: bfloat16 [256, 512], replicated, may hold values from -0.375 to 0.375
- w_in: bfloat16 [512, 1280], replicated, may hold values from -0.25 to 0.25
- w_out: bfloat16 [1024, 512], replicated, may hold values from -0.1875 to 0.1875
- skip: float32 [16], replicated, may hold values from 0.5 to 2
Outputs:
- grad_up: float32 [256, 512], replicated
- grad_in: float32 [512, 1280], replicated
- grad_out: float32 [1024, 512], replicated
- grad_skip: float32 [16], replicated
- grad_table: float32 [16384, 256], P(('batch', 'ctx'))
Inputs may be any that keep to these rules, and one draw needn't show every extreme that they name: `event_index`: rows are in blocks of 512; block k is held by device k of batch+ctx. The 256 events of one device name rows of at most 16 events in any one block, and in every draw some block is named by exactly 16 events of every device.
All inputs are finite; a program needn't handle non-finite values.
Results may differ from a plain program's by a relative error of at most 0.011.
Values may be sent and summed in bfloat16 or wider, within the bound.
A program may use at most 128 MiB of HBM per device.

v0:
```python
from functools import partial

import jax
import jax.numpy as jnp
from jax import lax
from jax.experimental import pallas as pl
from jax.experimental.pallas import tpu as pltpu
from jax.sharding import PartitionSpec as P

ROWS_DEV = 512
ROWS_BITS = 9
STEP_SIZE = 0.0625
LANES = 128
TILE = 16
MESH = pl.DeviceIdType.MESH
F32 = jnp.float32
BF16 = jnp.bfloat16
VMEM = pl.BlockSpec(memory_space=pltpu.VMEM)
SMEM = pl.BlockSpec(memory_space=pltpu.SMEM)
LIMIT = 48 * 1024 * 1024


def mm(a, b):
    return lax.dot_general(a, b, (((1,), (0,)), ((), ())), preferred_element_type=F32)


def mm_t(a, b):
    return lax.dot_general(a, b, (((1,), (1,)), ((), ())), preferred_element_type=F32)


def t_mm(a, b):
    return lax.dot_general(a, b, (((0,), (0,)), ((), ())), preferred_element_type=F32)


def exact_mm_t(a, b):
    return lax.dot_general(
        a, b, (((1,), (1,)), ((), ())), precision=lax.Precision.HIGHEST, preferred_element_type=F32
    )


def cut(j):
    return slice(LANES * j, LANES * (j + 1))


def front(cap, er, idx, decay, hs, dout, w_up, w_in, w_out, skip,
          u_out, x_out, b_out, dxl_out, tail_out, db_out, dc_out, sums_out, amount_out, gout_out,
          pick_out, tags_out, y_buf, dsk):
    tokens = er.shape[0]
    inner = w_out.shape[0]
    state = b_out.shape[1]
    heads = decay.shape[0]
    scale = state ** -0.5
    u = mm(er[...], w_up[...]).astype(BF16)
    u_out[...] = u
    proj = mm(u, w_in[...]).astype(BF16)
    x_out[...] = proj[:, :inner]
    b = proj[:, inner:inner + state]
    c = proj[:, inner + state:]
    b_out[...] = b
    dy = mm_t(dout[...], w_out[...]).astype(BF16)
    logs = jnp.log(decay[...])
    rows = lax.broadcasted_iota(jnp.int32, (tokens, tokens), 0)
    cols = lax.broadcasted_iota(jnp.int32, (tokens, tokens), 1)
    causal = rows >= cols
    tri = jnp.where(causal, 1.0, 0.0).astype(F32)
    cum_col = exact_mm_t(tri, logs)
    cum_row = exact_mm_t(logs, tri)
    total = cum_col[tokens - 1:tokens, :]
    start = jnp.exp(cum_col)
    tail = jnp.exp(total - cum_col)
    amount = jnp.exp(total)
    cb = jnp.where(causal, mm_t(c, b), 0.0)
    first = lax.broadcasted_iota(jnp.int32, (1, LANES), 1) < LANES // 2
    weight = jnp.zeros((tokens, tokens), F32)
    dc = jnp.zeros((tokens, state), F32)
    for j in range(heads // 2):
        xp = proj[:, cut(j)]
        dyp = dy[:, cut(j)]
        xf = xp.astype(F32)
        dyf = dyp.astype(F32)
        forward, backward = [], []
        prod = jnp.sum(xf * dyf, axis=0, keepdims=True)
        for i in range(2):
            h = 2 * j + i
            mine = first if i == 0 else jnp.logical_not(first)
            mask = jnp.exp(jnp.minimum(cum_col[:, h:h + 1] - cum_row[h:h + 1, :], 0.0))
            g = (mask * cb).astype(BF16)
            forward.append(mm(g, xp))
            backward.append(t_mm(g, dyp))
            weight += mask * mm_t(jnp.where(mine, dyf, 0.0).astype(BF16), xp)
            dsk[h:h + 1, :] = jnp.broadcast_to(
                jnp.sum(jnp.where(mine, prod, 0.0), axis=1, keepdims=True), (1, LANES))

        def spread(a):
            return jnp.where(first, a[:, 2 * j:2 * j + 1], a[:, 2 * j + 1:2 * j + 2])

        start_p = spread(start)
        skip_p = jnp.where(first, skip[2 * j], skip[2 * j + 1])
        hs_p = hs[LANES * j:LANES * (j + 1), :].astype(BF16)
        within = jnp.where(first, forward[0], forward[1])
        y = scale * (mm_t(c, hs_p) * start_p + STEP_SIZE * within) + skip_p * xf
        y_buf[:, cut(j)] = y.astype(BF16)
        dxl_out[:, cut(j)] = (STEP_SIZE * scale) * jnp.where(first, backward[0], backward[1]) + skip_p * dyf
        tail_out[:, cut(j)] = spread(tail)
        sdy = (start_p * dyf).astype(BF16)
        half, k = j // (heads // 4), j % (heads // 4)
        sums_out[half, :, cut(k)] = (scale * t_mm(c, sdy)).astype(BF16)
        amount_out[half, :, cut(k)] = jnp.broadcast_to(spread(amount), (8, LANES))
        dc += mm(sdy, hs_p)
    weight = jnp.where(causal, weight, 0.0).astype(BF16)
    dc_out[...] = scale * (dc + STEP_SIZE * mm(weight, b))
    db_out[...] = (STEP_SIZE * scale) * t_mm(weight, c)
    y_all = y_buf[...]
    for j in range(dout.shape[1] // LANES):
        gout_out[inner * j:inner * (j + 1), :] = t_mm(y_all, dout[:, cut(j)]).astype(BF16)
    route(cap, idx[...], dsk[...], pick_out, tags_out)


def route(cap, idx_row, value, pick_out, tags_out):
    slots, tokens = pick_out.shape
    spread = jnp.broadcast_to(idx_row.astype(F32), (LANES, tokens))
    idx_col = spread.T[:, 0:1].astype(jnp.int32)
    owner_row = lax.shift_right_logical(idx_row, ROWS_BITS)
    owner_col = lax.shift_right_logical(idx_col, ROWS_BITS)
    earlier = lax.broadcasted_iota(jnp.int32, (tokens, tokens), 0) < lax.broadcasted_iota(
        jnp.int32, (tokens, tokens), 1)
    rank = jnp.sum(
        jnp.where(jnp.logical_and(earlier, owner_col == owner_row), 1.0, 0.0), axis=0, keepdims=True)
    slot = owner_row * cap + rank.astype(jnp.int32)
    pick = jnp.where(
        lax.broadcasted_iota(jnp.int32, (slots, tokens), 0) == slot, 1.0, 0.0).astype(BF16)
    pick_out[...] = pick
    number = idx_col - owner_col * ROWS_DEV + 1
    high = lax.shift_right_logical(number, 8)
    low = number - high * 256
    lane = lax.broadcasted_iota(jnp.int32, (tokens, LANES), 1)
    tags = jnp.where(lane == 0, high.astype(F32), jnp.where(lane == 1, low.astype(F32), 0.0))
    one = value.astype(BF16).astype(F32)
    two = (value - one).astype(BF16).astype(F32)
    three = value - one - two
    place = lax.broadcasted_iota(jnp.int32, value.shape, 1)
    share = jnp.where(place == 2, one, jnp.where(place == 3, two, jnp.where(place == 4, three, 0.0)))
    if cap > share.shape[0]:
        share = jnp.concatenate([share, jnp.zeros((cap - share.shape[0], LANES), F32)], axis=0)
    tagged = mm(pick, tags.astype(BF16)).reshape(slots // cap, cap, LANES) + share[None]
    tags_out[...] = tagged.reshape(slots, LANES).astype(BF16)


def back(er, u, x, b, dxl, tail, db, dc, carry, w_in, grads_out):
    carry_all = jnp.concatenate([carry[0], carry[1]], axis=1)
    tail_v = tail[...]
    dx = dxl[...] + STEP_SIZE * tail_v * mm(b[...], carry_all)
    dbv = db[...] + STEP_SIZE * mm_t((tail_v * x[...].astype(F32)).astype(BF16), carry_all)
    dproj = jnp.concatenate([dx.astype(BF16), dbv.astype(BF16), dc[...].astype(BF16)], axis=1)
    du = mm_t(dproj, w_in[...]).astype(BF16)
    erv = er[...]
    width = erv.shape[1]
    for j in range(du.shape[1] // LANES):
        grads_out[width * j:width * (j + 1), :] = t_mm(erv, du[:, cut(j)]).astype(BF16)
    base = width * (du.shape[1] // LANES)
    uv = u[...]
    depth = uv.shape[1]
    for j in range(dproj.shape[1] // LANES):
        grads_out[base + depth * j:base + depth * (j + 1), :] = t_mm(uv, dproj[:, cut(j)]).astype(BF16)
    return du


def unpack(gout, grads, arrived, grad_up, grad_in, grad_out, grad_skip, grad_table):
    inner = grad_out.shape[0]
    for j in range(grad_out.shape[1] // LANES):
        grad_out[:, cut(j)] = gout[inner * j:inner * (j + 1), :].astype(F32)
    width, depth = grad_up.shape
    for j in range(depth // LANES):
        grad_up[:, cut(j)] = grads[width * j:width * (j + 1), :].astype(F32)
    base = width * (depth // LANES)
    for j in range(grad_in.shape[1] // LANES):
        grad_in[:, cut(j)] = grads[base + depth * j:base + depth * (j + 1), :].astype(F32)
    tags = arrived[:, width:].astype(F32)
    number = tags[:, 0:1] * 256.0 + tags[:, 1:2] - 1.0
    slots = tags.shape[0]
    row = lax.broadcasted_iota(jnp.int32, (slots, ROWS_DEV), 1).astype(F32)
    pick = jnp.where(row == number, 1.0, 0.0).astype(BF16)
    grad_table[...] = t_mm(pick, arrived[:, :width])
    heads = grad_skip.shape[1]
    cap = TILE
    parts = jnp.sum(tags.reshape(slots // cap, cap, LANES), axis=0)[:heads]
    place = lax.broadcasted_iota(jnp.int32, parts.shape, 1)
    kept = jnp.where(jnp.logical_and(place >= 2, place <= 4), parts, 0.0)
    sums = jnp.sum(kept, axis=1, keepdims=True)
    same = lax.broadcasted_iota(jnp.int32, (heads, heads), 0) == lax.broadcasted_iota(
        jnp.int32, (heads, heads), 1)
    grad_skip[...] = jnp.sum(jnp.where(same, sums, 0.0), axis=0, keepdims=True)


def bit_count(n):
    return n.bit_length() - 1


class Summing:
    def __init__(self, rows, batch_n, ctx_n):
        self.names = [("batch", i) for i in range(bit_count(batch_n))]
        self.names += [("ctx", i) for i in range(bit_count(ctx_n))]
        self.levels = len(self.names)
        tiles = rows // (batch_n * ctx_n) // TILE
        self.streams = []
        base = 0
        recv = 0
        rest = self.names[1:]
        for s in range(3):
            mine = (tiles + 2 - s) // 3
            if mine == 0:
                continue
            turn = rest[:3]
            order = self.names[:1] + turn[s:] + turn[:s] + rest[3:]
            size = mine * TILE << self.levels
            slots = []
            for k in range(self.levels):
                slots.append(recv)
                recv += size >> (k + 1)
            self.streams.append((base, size, order, slots))
            base += size
        self.recv_rows = recv
        self.sems = len(self.streams) * self.levels * 2

    def scratch(self, rows):
        return [
            pltpu.VMEM((rows, LANES), BF16),
            pltpu.VMEM((self.recv_rows, LANES), BF16),
            pltpu.VMEM((rows, LANES), BF16),
            pltpu.SemaphoreType.DMA((self.sems,)),
            pltpu.SemaphoreType.DMA((self.sems,)),
        ]

    def partners(self, where):
        out = []
        for axis, bit in self.names:
            out.append(self.partner(where, axis, bit)[0])
        return out

    def partner(self, where, axis, bit):
        at = where[axis]
        mine = (at // (1 << bit)) % 2
        other = at + (1 - 2 * mine) * (1 << bit)
        target = (other, where["ctx"]) if axis == "batch" else (where["batch"], other)
        return target, mine

    def bind(self, where, acc, recv, full, send_sem, recv_sem):
        self.acc, self.recv, self.full = acc, recv, full
        self.copies = []
        self.keeps = []
        for s, (base, size, order, slots) in enumerate(self.streams):
            off = base
            down, up, keeps = [], [], []
            for k, (axis, bit) in enumerate(order):
                target, mine = self.partner(where, axis, bit)
                half = size >> (k + 1)
                keep = pl.multiple_of(off + mine * half, TILE)
                away = pl.multiple_of(off + (1 - mine) * half, TILE)
                n = (s * self.levels + k) * 2
                down.append(pltpu.make_async_remote_copy(
                    src_ref=acc.at[pl.ds(away, half)], dst_ref=recv.at[pl.ds(slots[k], half)],
                    send_sem=send_sem.at[n], recv_sem=recv_sem.at[n],
                    device_id=target, device_id_type=MESH))
                up.append(pltpu.make_async_remote_copy(
                    src_ref=full.at[pl.ds(keep, half)], dst_ref=full.at[pl.ds(keep, half)],
                    send_sem=send_sem.at[n + 1], recv_sem=recv_sem.at[n + 1],
                    device_id=target, device_id_type=MESH))
                keeps.append((keep, half, slots[k]))
                off = keep
            self.copies.append((down, up))
            self.keeps.append(keeps)

    def begin(self):
        for down, _ in self.copies:
            down[0].start()

    def step(self, k):
        last = self.levels - 1
        for s, (down, up) in enumerate(self.copies):
            if k <= last:
                down[k].wait()
                keep, half, slot = self.keeps[s][k]
                total = self.acc[pl.ds(keep, half), :].astype(F32) + self.recv[pl.ds(slot, half), :].astype(F32)
                if k < last:
                    self.acc[pl.ds(keep, half), :] = total.astype(BF16)
                    down[k + 1].start()
                else:
                    self.full[pl.ds(keep, half), :] = total.astype(BF16)
                    up[last].start()
            else:
                n = 2 * self.levels - 1 - k
                up[n].wait()
                if n > 0:
                    up[n - 1].start()

    @property
    def steps(self):
        return 2 * self.levels


def position():
    return {"batch": lax.axis_index("batch"), "ctx": lax.axis_index("ctx")}


def middle(early, late, cap, batch_n, ctx_n,
           sums, amount, gout, pick, tags, er, u, x, b, dxl, tail, db, dc, w_up, w_in,
           gout_out, grads_out, arrived_out,
           e_acc, e_recv, e_full, e_send, e_got, l_acc, l_recv, l_full, l_send, l_got,
           other, other_amount, moving, entering, entering_other, carry, c_send, c_recv,
           rows, arrived, r_send, r_recv, own_sem):
    where = position()
    batch, ctx = where["batch"], where["ctx"]
    me = batch * ctx_n + ctx
    count = batch_n * ctx_n
    pair, place = ctx // 2, ctx % 2
    pairs = ctx_n // 2
    entering[...] = jnp.zeros_like(entering)
    partner = (batch, ctx + 1 - 2 * place)
    earlier = (batch, jnp.maximum(ctx - 2, 0))
    barrier = pltpu.get_barrier_semaphore()

    def at(step):
        to = (me + step) % count
        return to, (to // ctx_n, to % ctx_n)

    def hello(step, _):
        pl.semaphore_signal(barrier, inc=1, device_id=at(step)[1], device_id_type=MESH)
        return 0

    lax.fori_loop(1, count, hello, 0)
    e_acc[...] = gout[...]
    pl.semaphore_wait(barrier, count - 1)

    def send(src, dst, n, target):
        return pltpu.make_async_remote_copy(
            src_ref=src, dst_ref=dst, send_sem=c_send.at[n], recv_sem=c_recv.at[n],
            device_id=target, device_id_type=MESH)

    amounts = send(amount, other_amount, 0, partner)
    halves = send(sums.at[1 - place], other.at[1 - place], 1, partner)
    second = send(sums.at[1], other.at[1], 2, partner)
    hop = send(moving, entering, 3, earlier)
    cross = send(entering, entering_other, 4, partner)
    amounts.start()
    halves.start()

    early.bind(where, e_acc, e_recv, e_full, e_send, e_got)
    late.bind(where, l_acc, l_recv, l_full, l_send, l_got)
    early.begin()
    amounts.wait()
    halves.wait()

    @pl.when(place == 1)
    def _():
        second.start()

    mine = sums[place].astype(F32)
    theirs = other[place].astype(F32)
    a_mine = amount[place][0:1]
    a_theirs = other_amount[place][0:1]
    is_first = place == 0
    whole = jnp.where(is_first, mine + a_mine * theirs, theirs + a_theirs * mine)
    a_whole = a_mine * a_theirs
    done = 0
    for h in range(pairs - 2, -1, -1):
        @pl.when(pair == h + 1)
        def _():
            moving[...] = (whole + a_whole * entering[...].astype(F32)).astype(BF16)
            hop.start()

        if done < early.levels:
            early.step(done)
            done += 1

        @pl.when(pair == h)
        def _():
            hop.wait_recv()

    cross.start()
    early.step(done)
    done += 1
    cross.wait()

    @pl.when(place == 1)
    def _():
        second.wait_send()
        carry[1] = entering[...]
        carry[0] = entering_other[...]

    @pl.when(place == 0)
    def _():
        second.wait_recv()
        carry[0] = (other[0].astype(F32) + other_amount[0][0:1] * entering[...].astype(F32)).astype(BF16)
        carry[1] = (other[1].astype(F32) + other_amount[1][0:1] * entering_other[...].astype(F32)).astype(BF16)

    @pl.when(pair > 0)
    def _():
        hop.wait_send()

    du = back(er, u, x, b, dxl, tail, db, dc, carry, w_in, l_acc)
    late.begin()
    width = er.shape[1]
    rows[:, :width] = mm(pick[...], mm_t(du, w_up[...]).astype(BF16)).astype(BF16)
    rows[:, width:] = tags[...]
    own_rows = pl.ds(pl.multiple_of(me * cap, TILE), cap)
    own = pltpu.make_async_copy(rows.at[own_rows], arrived.at[own_rows], own_sem)
    own.start()

    def row_copy(step):
        to, target = at(step)
        return pltpu.make_async_remote_copy(
            src_ref=rows.at[pl.ds(pl.multiple_of(to * cap, TILE), cap)], dst_ref=arrived.at[own_rows],
            send_sem=r_send.at[step], recv_sem=r_recv.at[step],
            device_id=target, device_id_type=MESH)

    def launch(step, _):
        row_copy(step).start()
        return 0

    lax.fori_loop(1, count, launch, 0)
    for k in range(late.steps):
        late.step(k)
        if done < early.steps:
            early.step(done)
            done += 1
            if done == early.steps:
                gout_out[...] = e_full[...]

    def finish(step, _):
        row_copy(step).wait()
        return 0

    lax.fori_loop(1, count, finish, 0)
    own.wait()
    grads_out[...] = l_full[...]
    arrived_out[...] = arrived[...]


def local(event_rows, event_index, decay, saved_state, dout, w_up, w_in, w_out, skip):
    batch_n = lax.axis_size("batch")
    ctx_n = lax.axis_size("ctx")
    count = batch_n * ctx_n
    er = event_rows[0]
    tokens, width = er.shape
    inner, depth = w_out.shape
    proj = w_in.shape[1]
    state = (proj - inner) // 2
    heads = skip.shape[0]
    half = inner // 2
    cap = TILE
    shape = jax.ShapeDtypeStruct
    params = pltpu.CompilerParams(vmem_limit_bytes=LIMIT)
    gout_rows = inner * depth // LANES
    grad_rows = (width * depth + depth * proj) // LANES
    slots = count * cap
    held = jnp.swapaxes(saved_state[0, 0], 1, 2).reshape(inner, state)
    u, x, b, dxl, tail, db, dc, sums, amount, gout, pick, tags = pl.pallas_call(
        partial(front, cap),
        out_shape=(
            shape((tokens, depth), BF16), shape((tokens, inner), BF16), shape((tokens, state), BF16),
            shape((tokens, inner), F32), shape((tokens, inner), F32), shape((tokens, state), F32),
            shape((tokens, state), F32), shape((2, state, half), BF16), shape((2, 8, half), F32),
            shape((gout_rows, LANES), BF16), shape((slots, tokens), BF16), shape((slots, LANES), BF16),
        ),
        in_specs=[VMEM] * 8 + [SMEM],
        out_specs=[VMEM] * 12,
        scratch_shapes=[pltpu.VMEM((tokens, inner), BF16), pltpu.VMEM((heads, LANES), F32)],
        compiler_params=params,
        name="front",
    )(er, event_index, decay[0], held, dout[0], w_up, w_in, w_out, skip)

    early = Summing(gout_rows, batch_n, ctx_n)
    late = Summing(grad_rows, batch_n, ctx_n)
    gout, grads, arrived = pl.pallas_call(
        partial(middle, early, late, cap, batch_n, ctx_n),
        out_shape=(
            shape((gout_rows, LANES), BF16), shape((grad_rows, LANES), BF16),
            shape((slots, width + LANES), BF16),
        ),
        in_specs=[VMEM] * 15,
        out_specs=[VMEM] * 3,
        scratch_shapes=early.scratch(gout_rows) + late.scratch(grad_rows) + [
            pltpu.VMEM((2, state, half), BF16),
            pltpu.VMEM((2, 8, half), F32),
            pltpu.VMEM((state, half), BF16),
            pltpu.VMEM((state, half), BF16),
            pltpu.VMEM((state, half), BF16),
            pltpu.VMEM((2, state, half), BF16),
            pltpu.SemaphoreType.DMA((5,)),
            pltpu.SemaphoreType.DMA((5,)),
            pltpu.VMEM((slots, width + LANES), BF16),
            pltpu.VMEM((slots, width + LANES), BF16),
            pltpu.SemaphoreType.DMA((count,)),
            pltpu.SemaphoreType.DMA((count,)),
            pltpu.SemaphoreType.DMA,
        ],
        compiler_params=pltpu.CompilerParams(
            vmem_limit_bytes=LIMIT, collective_id=0, has_side_effects=True),
        name="middle",
    )(sums, amount, gout, pick, tags, er, u, x, b, dxl, tail, db, dc, w_up, w_in)

    grad_up, grad_in, grad_out, grad_skip, grad_table = pl.pallas_call(
        unpack,
        out_shape=(
            shape((width, depth), F32), shape((depth, proj), F32), shape((inner, depth), F32),
            shape((1, heads), F32), shape((ROWS_DEV, width), F32),
        ),
        in_specs=[VMEM] * 3,
        out_specs=[VMEM] * 5,
        compiler_params=params,
        name="unpack",
    )(gout, grads, arrived)
    return grad_up, grad_in, grad_out, grad_skip[0], grad_table


def solution(mesh):
    in_specs = (
        P("batch", "ctx", None),
        P("batch", "ctx"),
        P("batch", None, "ctx"),
        P("batch", "ctx", None, None, None),
        P("batch", "ctx", None),
        P(),
        P(),
        P(),
        P(),
    )
    out_specs = (P(), P(), P(), P(), P(("batch", "ctx"), None))
    return jax.shard_map(local, mesh=mesh, in_specs=in_specs, out_specs=out_specs, check_vma=False)
```

profile of v0, /device:TPU:0, one launch (start us, length us, event | category | flops | bytes accessed | tf_op | source)
XLA Modules:
  0.0 89.8 jit_solution(9005455909099760052)
XLA Ops:
  0.6 0.0 copy-start.2
  0.6 0.9 %copy-done.2 = bf16[256,512]{1,0:T(8,128)(2,1)S(1)} copy-done((bf16[256,512]{1,0:T(8,128)(2,1)S(1)}, bf16[256,512]{1,0:T(8,128)(2,1)}, u32[]{:S(2)}) %copy-start.2) | copy-done | bytes 262168
  1.6 0.0 copy-start.4
  1.6 0.9 %copy-done.4 = bf16[1,256,256]{2,1,0:T(8,128)(2,1)S(1)} copy-done((bf16[1,256,256]{2,1,0:T(8,128)(2,1)S(1)}, bf16[1,256,256]{2,1,0:T(8,128)(2,1)}, u32[]{:S(2)}) %copy-start.4) | copy-done | bytes 131096
  2.5 0.0 copy-start.5
  2.5 1.0 %copy-done.5 = f32[1,1,16,128,64]{3,4,2,1,0:T(8,128)S(1)} copy-done((f32[1,1,16,128,64]{3,4,2,1,0:T(8,128)S(1)}, f32[1,1,16,128,64]{3,4,2,1,0:T(8,128)}, u32[]{:S(2)}) %copy-start.5) | copy-done | bytes 524312
  3.5 0.0 copy-start.6
  3.5 0.9 %copy-done.6 = bf16[1,256,512]{2,1,0:T(8,128)(2,1)S(1)} copy-done((bf16[1,256,512]{2,1,0:T(8,128)(2,1)S(1)}, bf16[1,256,512]{2,1,0:T(8,128)(2,1)}, u32[]{:S(2)}) %copy-start.6) | copy-done | bytes 262168
  4.5 0.0 copy-start.7
  4.5 0.7 copy-done.7
  5.2 0.0 copy-start.8
  5.2 0.7 copy-done.8
  5.9 0.0 copy-start.9
  5.9 0.7 copy-done.9
  6.5 0.0 copy-start.3
  6.5 7.5 %front.1 = (bf16[256,512]{1,0:T(8,128)(2,1)S(1)}, bf16[256,1024]{1,0:T(8,128)(2,1)S(1)}, bf16[256,128]{1,0:T(8,128)(2,1)S(1)}, f32[256,1024]{1,0:T(8,128)S(1)}, ...) custom-call(bf16[256,256]{1,0:T(8,128)(2,1)S(1)} %bitcast.9, ...), custom_call_target="tpu_custom_call" | custom-call | tf_op jit(solution)/shard_map/front/pallas_call | solution.py:457
  14.1 0.0 copy-start.1
  14.1 1.0 %copy-done.1 = f32[256,1024]{1,0:T(8,128)} copy-done((f32[256,1024]{1,0:T(8,128)}, f32[256,1024]{1,0:T(8,128)S(1)}, u32[]{:S(2)}) %copy-start.1) | copy-done | bytes 1048600
  15.1 0.0 copy-done.3
  15.1 70.1 %middle.1 = (bf16[4096,128]{1,0:T(8,128)(2,1)S(1)}, bf16[6144,128]{1,0:T(8,128)(2,1)}, bf16[512,384]{1,0:T(8,128)(2,1)S(1)}) custom-call(bf16[2,128,512]{2,1,0:T(8,128)(2,1)S(1)} %get-tuple-element.25.sums, f32[2,8,512]{2,1,0:T(8,128)S(1)} %get-tuple-element.26.amount, bf16[4096,128]{1,0:T(8,128)(2,1)S(1)} %get-tuple-element.27.gout, ...), custom_call_target="tpu_custom_call" | custom-call | tf_op jit(solution)/shard_map/middle/pallas_call | solution.py:474
  85.2 0.0 copy-start
  85.2 1.4 %copy-done = bf16[6144,128]{1,0:T(8,128)(2,1)S(1)} copy-done((bf16[6144,128]{1,0:T(8,128)(2,1)S(1)}, bf16[6144,128]{1,0:T(8,128)(2,1)}, u32[]{:S(2)}) %copy-start) | copy-done | bytes 1572888
  86.6 3.2 %unpack.1 = (f32[256,512]{1,0:T(8,128)}, f32[512,1280]{1,0:T(8,128)}, f32[1024,512]{1,0:T(8,128)}, f32[1,16]{1,0:T(1,128)}, f32[512,256]{1,0:T(8,128)}) custom-call(bf16[4096,128]{1,0:T(8,128)(2,1)S(1)} %get-tuple-element.37.gout, bf16[6144,128]{1,0:T(8,128)(2,1)S(1)} %copy-done, bf16[512,384]{1,0:T(8,128)(2,1)S(1)} %get-tuple-element.39.arrived), custom_call_target="tpu_custom_call" | custom-call | tf_op jit(solution)/shard_map/unpack/pallas_call | solution.py:502
Async XLA Ops:
  0.6 1.0 %copy-start.2 = (bf16[256,512]{1,0:T(8,128)(2,1)S(1)}, bf16[256,512]{1,0:T(8,128)(2,1)}, u32[]{:S(2)}) copy-start(bf16[256,512]{1,0:T(8,128)(2,1)} %w_up.3) | copy-start | bytes 786436
  1.6 0.9 %copy-start.4 = (bf16[1,256,256]{2,1,0:T(8,128)(2,1)S(1)}, bf16[1,256,256]{2,1,0:T(8,128)(2,1)}, u32[]{:S(2)}) copy-start(bf16[1,256,256]{2,1,0:T(8,128)(2,1)} %param.9) | copy-start | bytes 393220
  2.5 1.0 %copy-start.5 = (f32[1,1,16,128,64]{3,4,2,1,0:T(8,128)S(1)}, f32[1,1,16,128,64]{3,4,2,1,0:T(8,128)}, u32[]{:S(2)}) copy-start(f32[1,1,16,128,64]{3,4,2,1,0:T(8,128)} %param.12) | copy-start | bytes 1572868
  3.5 0.9 %copy-start.6 = (bf16[1,256,512]{2,1,0:T(8,128)(2,1)S(1)}, bf16[1,256,512]{2,1,0:T(8,128)(2,1)}, u32[]{:S(2)}) copy-start(bf16[1,256,512]{2,1,0:T(8,128)(2,1)} %param.13) | copy-start | bytes 786436
  4.5 0.7 copy-start.7
  5.2 0.7 copy-start.8
  5.9 0.7 copy-start.9
  6.5 8.5 %copy-start.3 = (bf16[256,512]{1,0:T(8,128)(2,1)S(1)}, bf16[256,512]{1,0:T(8,128)(2,1)}, u32[]{:S(2)}) copy-start(bf16[256,512]{1,0:T(8,128)(2,1)} %w_up.3) | copy-start | bytes 786436
  14.1 1.0 %copy-start.1 = (f32[256,1024]{1,0:T(8,128)}, f32[256,1024]{1,0:T(8,128)S(1)}, u32[]{:S(2)}) copy-start(f32[256,1024]{1,0:T(8,128)S(1)} %get-tuple-element.34.tail) | copy-start | bytes 3145732
  85.2 1.4 %copy-start = (bf16[6144,128]{1,0:T(8,128)(2,1)S(1)}, bf16[6144,128]{1,0:T(8,128)(2,1)}, u32[]{:S(2)}) copy-start(bf16[6144,128]{1,0:T(8,128)(2,1)} %get-tuple-element.38.grads) | copy-start | bytes 4718596
where the time goes:
time: 90.2 us; the launch traced here: 89.8 us
  Pallas kernels  80.9 us (90%)
  local copies, waits for them, and re-layouts  8.26 us (9%)
    pallas_call x1, Pallas kernels, local(): pl.pallas_call(partial(middle, early, late, cap, batch_n, ctx_n), out_sha...  70.1 us
    unnamed x20, local copies, waits for them, and re-layouts  8.26 us
    pallas_call x1, Pallas kernels, local(): pl.pallas_call(partial(front, cap), out_shape=(shape((tokens, depth), BF1...  7.53 us
    pallas_call x1, Pallas kernels, local(): pl.pallas_call(unpack, out_shape=(shape((width, depth), F32), shape((dept...  3.19 us

commit v1 on v0

--- a/solution.py
+++ b/solution.py
@@ -17,7 +17,7 @@
 BF16 = jnp.bfloat16
 VMEM = pl.BlockSpec(memory_space=pltpu.VMEM)
 SMEM = pl.BlockSpec(memory_space=pltpu.SMEM)
-LIMIT = 48 * 1024 * 1024
+LIMIT = 60 * 1024 * 1024
 
 
 def mm(a, b):
@@ -42,9 +42,7 @@
     return slice(LANES * j, LANES * (j + 1))
 
 
-def front(cap, er, idx, decay, hs, dout, w_up, w_in, w_out, skip,
-          u_out, x_out, b_out, dxl_out, tail_out, db_out, dc_out, sums_out, amount_out, gout_out,
-          pick_out, tags_out, y_buf, dsk):
+def front(er, decay, dout, w_up, w_in, w_out, u_out, x_out, b_out, tail_out, sums_out, amount_out):
     tokens = er.shape[0]
     inner = w_out.shape[0]
     state = b_out.shape[1]
@@ -69,8 +67,31 @@
     start = jnp.exp(cum_col)
     tail = jnp.exp(total - cum_col)
     amount = jnp.exp(total)
+    first = lax.broadcasted_iota(jnp.int32, (1, LANES), 1) < LANES // 2
+    starts, sdys = [], []
+    for j in range(heads // 2):
+        def spread(a):
+            return jnp.where(first, a[:, 2 * j:2 * j + 1], a[:, 2 * j + 1:2 * j + 2])
+
+        starts.append(spread(start))
+        tail_out[:, cut(j)] = spread(tail)
+        sdy = (starts[j] * dy[:, cut(j)].astype(F32)).astype(BF16)
+        sdys.append(sdy)
+        half, k = j // (heads // 4), j % (heads // 4)
+        sums_out[half, :, cut(k)] = (scale * t_mm(c, sdy)).astype(BF16)
+        amount_out[half, :, cut(k)] = jnp.broadcast_to(spread(amount), (8, LANES))
+    return proj, dy, cum_col, cum_row, causal, first, starts, sdys
+
+
+def within(kept, hs, dout, skip, inner, dxl_out, db_out, dc_out, gout_out, y_buf, dsk):
+    proj, dy, cum_col, cum_row, causal, first, starts, sdys = kept
+    tokens = proj.shape[0]
+    heads = cum_row.shape[0]
+    state = db_out.shape[1]
+    scale = state ** -0.5
+    b = proj[:, inner:inner + state]
+    c = proj[:, inner + state:]
     cb = jnp.where(causal, mm_t(c, b), 0.0)
-    first = lax.broadcasted_iota(jnp.int32, (1, LANES), 1) < LANES // 2
     weight = jnp.zeros((tokens, tokens), F32)
     dc = jnp.zeros((tokens, state), F32)
     for j in range(heads // 2):
@@ -90,34 +111,23 @@
             weight += mask * mm_t(jnp.where(mine, dyf, 0.0).astype(BF16), xp)
             dsk[h:h + 1, :] = jnp.broadcast_to(
                 jnp.sum(jnp.where(mine, prod, 0.0), axis=1, keepdims=True), (1, LANES))
-
-        def spread(a):
-            return jnp.where(first, a[:, 2 * j:2 * j + 1], a[:, 2 * j + 1:2 * j + 2])
-
-        start_p = spread(start)
         skip_p = jnp.where(first, skip[2 * j], skip[2 * j + 1])
         hs_p = hs[LANES * j:LANES * (j + 1), :].astype(BF16)
-        within = jnp.where(first, forward[0], forward[1])
-        y = scale * (mm_t(c, hs_p) * start_p + STEP_SIZE * within) + skip_p * xf
+        inside = jnp.where(first, forward[0], forward[1])
+        y = scale * (mm_t(c, hs_p) * starts[j] + STEP_SIZE * inside) + skip_p * xf
         y_buf[:, cut(j)] = y.astype(BF16)
         dxl_out[:, cut(j)] = (STEP_SIZE * scale) * jnp.where(first, backward[0], backward[1]) + skip_p * dyf
-        tail_out[:, cut(j)] = spread(tail)
-        sdy = (start_p * dyf).astype(BF16)
-        half, k = j // (heads // 4), j % (heads // 4)
-        sums_out[half, :, cut(k)] = (scale * t_mm(c, sdy)).astype(BF16)
-        amount_out[half, :, cut(k)] = jnp.broadcast_to(spread(amount), (8, LANES))
-        dc += mm(sdy, hs_p)
+        dc += mm(sdys[j], hs_p)
     weight = jnp.where(causal, weight, 0.0).astype(BF16)
     dc_out[...] = scale * (dc + STEP_SIZE * mm(weight, b))
     db_out[...] = (STEP_SIZE * scale) * t_mm(weight, c)
     y_all = y_buf[...]
     for j in range(dout.shape[1] // LANES):
         gout_out[inner * j:inner * (j + 1), :] = t_mm(y_all, dout[:, cut(j)]).astype(BF16)
-    route(cap, idx[...], dsk[...], pick_out, tags_out)
-
-
-def route(cap, idx_row, value, pick_out, tags_out):
-    slots, tokens = pick_out.shape
+
+
+def route(cap, slots, idx_row, value):
+    tokens = idx_row.shape[1]
     spread = jnp.broadcast_to(idx_row.astype(F32), (LANES, tokens))
     idx_col = spread.T[:, 0:1].astype(jnp.int32)
     owner_row = lax.shift_right_logical(idx_row, ROWS_BITS)
@@ -129,7 +139,6 @@
     slot = owner_row * cap + rank.astype(jnp.int32)
     pick = jnp.where(
         lax.broadcasted_iota(jnp.int32, (slots, tokens), 0) == slot, 1.0, 0.0).astype(BF16)
-    pick_out[...] = pick
     number = idx_col - owner_col * ROWS_DEV + 1
     high = lax.shift_right_logical(number, 8)
     low = number - high * 256
@@ -143,7 +152,7 @@
     if cap > share.shape[0]:
         share = jnp.concatenate([share, jnp.zeros((cap - share.shape[0], LANES), F32)], axis=0)
     tagged = mm(pick, tags.astype(BF16)).reshape(slots // cap, cap, LANES) + share[None]
-    tags_out[...] = tagged.reshape(slots, LANES).astype(BF16)
+    return pick, tagged.reshape(slots, LANES).astype(BF16)
 
 
 def back(er, u, x, b, dxl, tail, db, dc, carry, w_in, grads_out):
@@ -303,8 +312,9 @@
 
 
 def middle(early, late, cap, batch_n, ctx_n,
-           sums, amount, gout, pick, tags, er, u, x, b, dxl, tail, db, dc, w_up, w_in,
+           er, idx, decay, hs, dout, w_up, w_in, w_out, skip,
            gout_out, grads_out, arrived_out,
+           sums, amount, u, x, b, dxl, tail, db, dc, y_buf, dsk, pick_buf,
            e_acc, e_recv, e_full, e_send, e_got, l_acc, l_recv, l_full, l_send, l_got,
            other, other_amount, moving, entering, entering_other, carry, c_send, c_recv,
            rows, arrived, r_send, r_recv, own_sem):
@@ -328,7 +338,7 @@
         return 0
 
     lax.fori_loop(1, count, hello, 0)
-    e_acc[...] = gout[...]
+    kept = front(er, decay, dout, w_up, w_in, w_out, u, x, b, tail, sums, amount)
     pl.semaphore_wait(barrier, count - 1)
 
     def send(src, dst, n, target):
@@ -346,7 +356,12 @@
 
     early.bind(where, e_acc, e_recv, e_full, e_send, e_got)
     late.bind(where, l_acc, l_recv, l_full, l_send, l_got)
+    within(kept, hs, dout, skip, w_out.shape[0], dxl, db, dc, e_acc, y_buf, dsk)
     early.begin()
+    width = er.shape[1]
+    pick, tags = route(cap, rows.shape[0], idx[...], dsk[...])
+    pick_buf[...] = pick
+    rows[:, width:] = tags
     amounts.wait()
     halves.wait()
 
@@ -399,9 +414,7 @@
 
     du = back(er, u, x, b, dxl, tail, db, dc, carry, w_in, l_acc)
     late.begin()
-    width = er.shape[1]
-    rows[:, :width] = mm(pick[...], mm_t(du, w_up[...]).astype(BF16)).astype(BF16)
-    rows[:, width:] = tags[...]
+    rows[:, :width] = mm(pick_buf[...], mm_t(du, w_up[...]).astype(BF16)).astype(BF16)
     own_rows = pl.ds(pl.multiple_of(me * cap, TILE), cap)
     own = pltpu.make_async_copy(rows.at[own_rows], arrived.at[own_rows], own_sem)
     own.start()
@@ -454,21 +467,6 @@
     grad_rows = (width * depth + depth * proj) // LANES
     slots = count * cap
     held = jnp.swapaxes(saved_state[0, 0], 1, 2).reshape(inner, state)
-    u, x, b, dxl, tail, db, dc, sums, amount, gout, pick, tags = pl.pallas_call(
-        partial(front, cap),
-        out_shape=(
-            shape((tokens, depth), BF16), shape((tokens, inner), BF16), shape((tokens, state), BF16),
-            shape((tokens, inner), F32), shape((tokens, inner), F32), shape((tokens, state), F32),
-            shape((tokens, state), F32), shape((2, state, half), BF16), shape((2, 8, half), F32),
-            shape((gout_rows, LANES), BF16), shape((slots, tokens), BF16), shape((slots, LANES), BF16),
-        ),
-        in_specs=[VMEM] * 8 + [SMEM],
-        out_specs=[VMEM] * 12,
-        scratch_shapes=[pltpu.VMEM((tokens, inner), BF16), pltpu.VMEM((heads, LANES), F32)],
-        compiler_params=params,
-        name="front",
-    )(er, event_index, decay[0], held, dout[0], w_up, w_in, w_out, skip)
-
     early = Summing(gout_rows, batch_n, ctx_n)
     late = Summing(grad_rows, batch_n, ctx_n)
     gout, grads, arrived = pl.pallas_call(
@@ -477,9 +475,22 @@
             shape((gout_rows, LANES), BF16), shape((grad_rows, LANES), BF16),
             shape((slots, width + LANES), BF16),
         ),
-        in_specs=[VMEM] * 15,
+        in_specs=[VMEM] * 8 + [SMEM],
         out_specs=[VMEM] * 3,
-        scratch_shapes=early.scratch(gout_rows) + late.scratch(grad_rows) + [
+        scratch_shapes=[
+            pltpu.VMEM((2, state, half), BF16),
+            pltpu.VMEM((2, 8, half), F32),
+            pltpu.VMEM((tokens, depth), BF16),
+            pltpu.VMEM((tokens, inner), BF16),
+            pltpu.VMEM((tokens, state), BF16),
+            pltpu.VMEM((tokens, inner), F32),
+            pltpu.VMEM((tokens, inner), F32),
+            pltpu.VMEM((tokens, state), F32),
+            pltpu.VMEM((tokens, state), F32),
+            pltpu.VMEM((tokens, inner), BF16),
+            pltpu.VMEM((heads, LANES), F32),
+            pltpu.VMEM((slots, tokens), BF16),
+        ] + early.scratch(gout_rows) + late.scratch(grad_rows) + [
             pltpu.VMEM((2, state, half), BF16),
             pltpu.VMEM((2, 8, half), F32),
             pltpu.VMEM((state, half), BF16),
@@ -497,7 +508,7 @@
         compiler_params=pltpu.CompilerParams(
             vmem_limit_bytes=LIMIT, collective_id=0, has_side_effects=True),
         name="middle",
-    )(sums, amount, gout, pick, tags, er, u, x, b, dxl, tail, db, dc, w_up, w_in)
+    )(er, event_index, decay[0], held, dout[0], w_up, w_in, w_out, skip)
 
     grad_up, grad_in, grad_out, grad_skip, grad_table = pl.pallas_call(
         unpack,

time: 90.2 us -> 79.7 us (0.88)
  local copies, waits for them, and re-layouts: 8.26 us -> 0 us
  Pallas kernels: 80.9 us -> 78.8 us
    unnamed x20 -> x0, local copies, waits for them, and re-layouts: 8.26 us -> none
    pallas_call x1 -> x0, Pallas kernels: 7.53 us -> none  [local(): pl.pallas_call(partial(front, cap), out_shape=(shape((tokens, depth), BF1...]
    pallas_call x1, Pallas kernels: 70.1 us -> 73.9 us  [local(): pl.pallas_call(partial(middle, early, late, cap, batch_n, ctx_n), out_sha...]
    pallas_call x1, Pallas kernels: 3.19 us -> 4.99 us  [local(): pl.pallas_call(unpack, out_shape=(shape((width, depth), F32), shape((dept...]
where the time goes in v1:
time: 79.7 us; the launch traced here: 79.5 us
  Pallas kernels  78.8 us (99%)
    pallas_call x1, Pallas kernels, local(): pl.pallas_call(partial(middle, early, late, cap, batch_n, ctx_n), out_sha...  73.9 us
    pallas_call x1, Pallas kernels, local(): pl.pallas_call(unpack, out_shape=(shape((width, depth), F32), shape((dept...  4.99 us

profile of v1, /device:TPU:0, one launch (start us, length us, event | category | flops | bytes accessed | tf_op | source)
XLA Modules:
  0.0 79.5 jit_solution(5212096238005100279)
XLA Ops:
  0.6 73.9 %middle.1 = (bf16[4096,128]{1,0:T(8,128)(2,1)}, bf16[6144,128]{1,0:T(8,128)(2,1)}, bf16[512,384]{1,0:T(8,128)(2,1)}) custom-call(bf16[256,256]{1,0:T(8,128)(2,1)} %bitcast.11, s32[1,256]{1,0:T(1,128)} %idx.1, f32[16,256]{1,0:T(8,128)} %bitcast.12, f32[1024,128]{1,0:T(8,128)} %bitcast.9, bf16[256,512]{1,0:T(8,128)(2,1)} %bitcast.10, bf16[256,512]{1,0:T(8,128)(2,1)} %w_up.1, ...), custom_call_target="tpu_custom_call" | custom-call | tf_op jit(solution)/shard_map/middle/pallas_call | solution.py:472
  74.5 5.0 %unpack.1 = (f32[256,512]{1,0:T(8,128)}, f32[512,1280]{1,0:T(8,128)}, f32[1024,512]{1,0:T(8,128)}, f32[1,16]{1,0:T(1,128)}, f32[512,256]{1,0:T(8,128)}) custom-call(bf16[4096,128]{1,0:T(8,128)(2,1)} %get-tuple-element.13.gout, bf16[6144,128]{1,0:T(8,128)(2,1)} %get-tuple-element.14.grads, bf16[512,384]{1,0:T(8,128)(2,1)} %get-tuple-element.15.arrived), custom_call_target="tpu_custom_call" | custom-call | tf_op jit(solution)/shard_map/unpack/pallas_call | solution.py:513

commit v2 on v1

--- a/solution.py
+++ b/solution.py
@@ -155,12 +155,13 @@
     return pick, tagged.reshape(slots, LANES).astype(BF16)
 
 
-def back(er, u, x, b, dxl, tail, db, dc, carry, w_in, grads_out):
+def back(beside, er, u, x, b, dxl, tail, db, dc, carry, w_in, grads_out):
     carry_all = jnp.concatenate([carry[0], carry[1]], axis=1)
     tail_v = tail[...]
     dx = dxl[...] + STEP_SIZE * tail_v * mm(b[...], carry_all)
     dbv = db[...] + STEP_SIZE * mm_t((tail_v * x[...].astype(F32)).astype(BF16), carry_all)
     dproj = jnp.concatenate([dx.astype(BF16), dbv.astype(BF16), dc[...].astype(BF16)], axis=1)
+    beside()
     du = mm_t(dproj, w_in[...]).astype(BF16)
     erv = er[...]
     width = erv.shape[1]
@@ -207,29 +208,35 @@
 
 class Summing:
     def __init__(self, rows, batch_n, ctx_n):
-        self.names = [("batch", i) for i in range(bit_count(batch_n))]
-        self.names += [("ctx", i) for i in range(bit_count(ctx_n))]
-        self.levels = len(self.names)
+        names = [("batch", i) for i in range(bit_count(batch_n))]
+        names += [("ctx", i) for i in range(bit_count(ctx_n))]
+        rest = names[1:]
+        self.levels = len(names) - 1
         tiles = rows // (batch_n * ctx_n) // TILE
         self.streams = []
         base = 0
         recv = 0
-        rest = self.names[1:]
+        self.sems = 0
         for s in range(3):
             mine = (tiles + 2 - s) // 3
             if mine == 0:
                 continue
             turn = rest[:3]
-            order = self.names[:1] + turn[s:] + turn[:s] + rest[3:]
-            size = mine * TILE << self.levels
-            slots = []
-            for k in range(self.levels):
-                slots.append(recv)
-                recv += size >> (k + 1)
-            self.streams.append((base, size, order, slots))
+            turn = turn[s:] + turn[:s]
+            groups = [names[:1], turn[:1], turn[1:2], turn[2:3] + rest[3:4]]
+            groups += [[name] for name in rest[4:]]
+            size = mine * TILE << len(names)
+            plan = []
+            part = size
+            for group in groups:
+                part //= 1 << len(group)
+                others = (1 << len(group)) - 1
+                plan.append((group, part, recv, self.sems))
+                recv += part * others
+                self.sems += 2 * others
+            self.streams.append((base, plan))
             base += size
         self.recv_rows = recv
-        self.sems = len(self.streams) * self.levels * 2
 
     def scratch(self, rows):
         return [
@@ -240,71 +247,77 @@
             pltpu.SemaphoreType.DMA((self.sems,)),
         ]
 
-    def partners(self, where):
-        out = []
-        for axis, bit in self.names:
-            out.append(self.partner(where, axis, bit)[0])
-        return out
-
-    def partner(self, where, axis, bit):
-        at = where[axis]
-        mine = (at // (1 << bit)) % 2
-        other = at + (1 - 2 * mine) * (1 << bit)
-        target = (other, where["ctx"]) if axis == "batch" else (where["batch"], other)
-        return target, mine
-
     def bind(self, where, acc, recv, full, send_sem, recv_sem):
         self.acc, self.recv, self.full = acc, recv, full
         self.copies = []
         self.keeps = []
-        for s, (base, size, order, slots) in enumerate(self.streams):
+        for base, plan in self.streams:
             off = base
             down, up, keeps = [], [], []
-            for k, (axis, bit) in enumerate(order):
-                target, mine = self.partner(where, axis, bit)
-                half = size >> (k + 1)
-                keep = pl.multiple_of(off + mine * half, TILE)
-                away = pl.multiple_of(off + (1 - mine) * half, TILE)
-                n = (s * self.levels + k) * 2
-                down.append(pltpu.make_async_remote_copy(
-                    src_ref=acc.at[pl.ds(away, half)], dst_ref=recv.at[pl.ds(slots[k], half)],
-                    send_sem=send_sem.at[n], recv_sem=recv_sem.at[n],
-                    device_id=target, device_id_type=MESH))
-                up.append(pltpu.make_async_remote_copy(
-                    src_ref=full.at[pl.ds(keep, half)], dst_ref=full.at[pl.ds(keep, half)],
-                    send_sem=send_sem.at[n + 1], recv_sem=recv_sem.at[n + 1],
-                    device_id=target, device_id_type=MESH))
-                keeps.append((keep, half, slots[k]))
+            for group, part, slot, sem in plan:
+                members = 1 << len(group)
+                bits = [(where[axis] // (1 << bit)) % 2 for axis, bit in group]
+                mine = sum(value * (1 << n) for n, value in enumerate(bits))
+                keep = pl.multiple_of(off + mine * part, TILE)
+                downs, ups = [], []
+                for d in range(1, members):
+                    member = (mine + d) % members
+                    at = dict(where)
+                    for n, (axis, bit) in enumerate(group):
+                        at[axis] = at[axis] + ((member // (1 << n)) % 2 - bits[n]) * (1 << bit)
+                    target = (at["batch"], at["ctx"])
+                    away = pl.multiple_of(off + member * part, TILE)
+                    n = sem + 2 * (d - 1)
+                    downs.append(pltpu.make_async_remote_copy(
+                        src_ref=acc.at[pl.ds(away, part)],
+                        dst_ref=recv.at[pl.ds(slot + (d - 1) * part, part)],
+                        send_sem=send_sem.at[n], recv_sem=recv_sem.at[n],
+                        device_id=target, device_id_type=MESH))
+                    ups.append(pltpu.make_async_remote_copy(
+                        src_ref=full.at[pl.ds(keep, part)], dst_ref=full.at[pl.ds(keep, part)],
+                        send_sem=send_sem.at[n + 1], recv_sem=recv_sem.at[n + 1],
+                        device_id=target, device_id_type=MESH))
+                down.append(downs)
+                up.append(ups)
+                keeps.append((keep, part, slot))
                 off = keep
             self.copies.append((down, up))
             self.keeps.append(keeps)
 
     def begin(self):
         for down, _ in self.copies:
-            down[0].start()
+            for copy in down[0]:
+                copy.start()
 
     def step(self, k):
         last = self.levels - 1
         for s, (down, up) in enumerate(self.copies):
             if k <= last:
-                down[k].wait()
-                keep, half, slot = self.keeps[s][k]
-                total = self.acc[pl.ds(keep, half), :].astype(F32) + self.recv[pl.ds(slot, half), :].astype(F32)
+                keep, part, slot = self.keeps[s][k]
+                total = self.acc[pl.ds(keep, part), :].astype(F32)
+                for n, copy in enumerate(down[k]):
+                    copy.wait()
+                    total += self.recv[pl.ds(slot + n * part, part), :].astype(F32)
                 if k < last:
-                    self.acc[pl.ds(keep, half), :] = total.astype(BF16)
-                    down[k + 1].start()
+                    self.acc[pl.ds(keep, part), :] = total.astype(BF16)
                 else:
-                    self.full[pl.ds(keep, half), :] = total.astype(BF16)
-                    up[last].start()
+                    self.full[pl.ds(keep, part), :] = total.astype(BF16)
+                following = down[k + 1] if k < last else up[last]
             else:
                 n = 2 * self.levels - 1 - k
-                up[n].wait()
-                if n > 0:
-                    up[n - 1].start()
+                for copy in up[n]:
+                    copy.wait()
+                following = up[n - 1] if n > 0 else []
+            for copy in following:
+                copy.start()
 
     @property
     def steps(self):
         return 2 * self.levels
+
+
+def joined(ref):
+    return jnp.concatenate([ref[n] for n in range(ref.shape[0])], axis=1)
 
 
 def position():
@@ -317,7 +330,7 @@
            sums, amount, u, x, b, dxl, tail, db, dc, y_buf, dsk, pick_buf,
            e_acc, e_recv, e_full, e_send, e_got, l_acc, l_recv, l_full, l_send, l_got,
            other, other_amount, moving, entering, entering_other, carry, c_send, c_recv,
-           rows, arrived, r_send, r_recv, own_sem):
+           rows, arrived, r_send, r_recv, own_sem, out_sems):
     where = position()
     batch, ctx = where["batch"], where["ctx"]
     me = batch * ctx_n + ctx
@@ -349,7 +362,8 @@
     amounts = send(amount, other_amount, 0, partner)
     halves = send(sums.at[1 - place], other.at[1 - place], 1, partner)
     second = send(sums.at[1], other.at[1], 2, partner)
-    hop = send(moving, entering, 3, earlier)
+    hops = [send(moving.at[n], entering.at[n], 5 + n, earlier) for n in range(entering.shape[0])]
+    span = entering.shape[2]
     cross = send(entering, entering_other, 4, partner)
     amounts.start()
     halves.start()
@@ -380,15 +394,20 @@
     for h in range(pairs - 2, -1, -1):
         @pl.when(pair == h + 1)
         def _():
-            moving[...] = (whole + a_whole * entering[...].astype(F32)).astype(BF16)
-            hop.start()
+            for n, hop in enumerate(hops):
+                if h + 1 < pairs - 1:
+                    hop.wait_recv()
+                piece = slice(n * span, (n + 1) * span)
+                moving[n] = (whole[:, piece] + a_whole[:, piece] * entering[n].astype(F32)).astype(BF16)
+                hop.start()
 
         if done < early.levels:
             early.step(done)
             done += 1
 
-        @pl.when(pair == h)
-        def _():
+    @pl.when(pair == 0)
+    def _():
+        for hop in hops:
             hop.wait_recv()
 
     cross.start()
@@ -399,20 +418,22 @@
     @pl.when(place == 1)
     def _():
         second.wait_send()
-        carry[1] = entering[...]
-        carry[0] = entering_other[...]
+        carry[1] = joined(entering)
+        carry[0] = joined(entering_other)
 
     @pl.when(place == 0)
     def _():
         second.wait_recv()
-        carry[0] = (other[0].astype(F32) + other_amount[0][0:1] * entering[...].astype(F32)).astype(BF16)
-        carry[1] = (other[1].astype(F32) + other_amount[1][0:1] * entering_other[...].astype(F32)).astype(BF16)
+        carry[0] = (other[0].astype(F32) + other_amount[0][0:1] * joined(entering).astype(F32)).astype(BF16)
+        carry[1] = (other[1].astype(F32) + other_amount[1][0:1] * joined(entering_other).astype(F32)).astype(BF16)
 
     @pl.when(pair > 0)
     def _():
-        hop.wait_send()
-
-    du = back(er, u, x, b, dxl, tail, db, dc, carry, w_in, l_acc)
+        for hop in hops:
+            hop.wait_send()
+
+    du = back(lambda: early.step(done), er, u, x, b, dxl, tail, db, dc, carry, w_in, l_acc)
+    done += 1
     late.begin()
     rows[:, :width] = mm(pick_buf[...], mm_t(du, w_up[...]).astype(BF16)).astype(BF16)
     own_rows = pl.ds(pl.multiple_of(me * cap, TILE), cap)
@@ -431,22 +452,28 @@
         return 0
 
     lax.fori_loop(1, count, launch, 0)
+    gout_copy = pltpu.make_async_copy(e_full, gout_out, out_sems.at[0])
+    grads_copy = pltpu.make_async_copy(l_full, grads_out, out_sems.at[1])
+    rows_done = pltpu.make_async_copy(arrived, arrived_out, out_sems.at[2])
     for k in range(late.steps):
         late.step(k)
         if done < early.steps:
             early.step(done)
             done += 1
             if done == early.steps:
-                gout_out[...] = e_full[...]
+                gout_copy.start()
 
     def finish(step, _):
         row_copy(step).wait()
         return 0
 
+    grads_copy.start()
     lax.fori_loop(1, count, finish, 0)
     own.wait()
-    grads_out[...] = l_full[...]
-    arrived_out[...] = arrived[...]
+    rows_done.start()
+    gout_copy.wait()
+    grads_copy.wait()
+    rows_done.wait()
 
 
 def local(event_rows, event_index, decay, saved_state, dout, w_up, w_in, w_out, skip):
@@ -476,7 +503,7 @@
             shape((slots, width + LANES), BF16),
         ),
         in_specs=[VMEM] * 8 + [SMEM],
-        out_specs=[VMEM] * 3,
+        out_specs=[pl.BlockSpec(memory_space=pl.ANY)] * 3,
         scratch_shapes=[
             pltpu.VMEM((2, state, half), BF16),
             pltpu.VMEM((2, 8, half), F32),
@@ -493,17 +520,18 @@
         ] + early.scratch(gout_rows) + late.scratch(grad_rows) + [
             pltpu.VMEM((2, state, half), BF16),
             pltpu.VMEM((2, 8, half), F32),
-            pltpu.VMEM((state, half), BF16),
-            pltpu.VMEM((state, half), BF16),
-            pltpu.VMEM((state, half), BF16),
+            pltpu.VMEM((2, state, half // 2), BF16),
+            pltpu.VMEM((2, state, half // 2), BF16),
+            pltpu.VMEM((2, state, half // 2), BF16),
             pltpu.VMEM((2, state, half), BF16),
-            pltpu.SemaphoreType.DMA((5,)),
-            pltpu.SemaphoreType.DMA((5,)),
+            pltpu.SemaphoreType.DMA((7,)),
+            pltpu.SemaphoreType.DMA((7,)),
             pltpu.VMEM((slots, width + LANES), BF16),
             pltpu.VMEM((slots, width + LANES), BF16),
             pltpu.SemaphoreType.DMA((count,)),
             pltpu.SemaphoreType.DMA((count,)),
             pltpu.SemaphoreType.DMA,
+            pltpu.SemaphoreType.DMA((3,)),
         ],
         compiler_params=pltpu.CompilerParams(
             vmem_limit_bytes=LIMIT, collective_id=0, has_side_effects=True),

time: 79.7 us -> 76.7 us (0.962)
  Pallas kernels: 78.8 us -> 75.9 us
    pallas_call x1, Pallas kernels: 73.9 us -> 70.9 us  [local(): pl.pallas_call(partial(middle, early, late, cap, batch_n, ctx_n), out_sha...]
where the time goes in v2:
time: 76.7 us; the launch traced here: 76.5 us
  Pallas kernels  75.9 us (99%)
    pallas_call x1, Pallas kernels, local(): pl.pallas_call(partial(middle, early, late, cap, batch_n, ctx_n), out_sha...  70.9 us
    pallas_call x1, Pallas kernels, local(): pl.pallas_call(unpack, out_shape=(shape((width, depth), F32), shape((dept...  4.99 us

profile of v2, /device:TPU:0, one launch (start us, length us, event | category | flops | bytes accessed | tf_op | source)
XLA Modules:
  0.0 76.5 jit_solution(6187787358852661964)
XLA Ops:
  0.6 70.9 %middle.1 = (bf16[4096,128]{1,0:T(8,128)(2,1)}, bf16[6144,128]{1,0:T(8,128)(2,1)}, bf16[512,384]{1,0:T(8,128)(2,1)}) custom-call(bf16[256,256]{1,0:T(8,128)(2,1)} %bitcast.11, s32[1,256]{1,0:T(1,128)} %idx.1, f32[16,256]{1,0:T(8,128)} %bitcast.12, f32[1024,128]{1,0:T(8,128)} %bitcast.9, bf16[256,512]{1,0:T(8,128)(2,1)} %bitcast.10, bf16[256,512]{1,0:T(8,128)(2,1)} %w_up.1, ...), custom_call_target="tpu_custom_call" | custom-call | tf_op jit(solution)/shard_map/middle/pallas_call | solution.py:499
  71.5 5.0 %unpack.1 = (f32[256,512]{1,0:T(8,128)}, f32[512,1280]{1,0:T(8,128)}, f32[1024,512]{1,0:T(8,128)}, f32[1,16]{1,0:T(1,128)}, f32[512,256]{1,0:T(8,128)}) custom-call(bf16[4096,128]{1,0:T(8,128)(2,1)} %get-tuple-element.13.gout, bf16[6144,128]{1,0:T(8,128)(2,1)} %get-tuple-element.14.grads, bf16[512,384]{1,0:T(8,128)(2,1)} %get-tuple-element.15.arrived), custom_call_target="tpu_custom_call" | custom-call | tf_op jit(solution)/shard_map/unpack/pallas_call | solution.py:541

commit v3 on v2

--- a/solution.py
+++ b/solution.py
@@ -155,42 +155,60 @@
     return pick, tagged.reshape(slots, LANES).astype(BF16)
 
 
-def back(beside, er, u, x, b, dxl, tail, db, dc, carry, w_in, grads_out):
+def back(late, beside, er, u, x, b, dxl, tail, db, dc, carry, w_in, grads_out):
     carry_all = jnp.concatenate([carry[0], carry[1]], axis=1)
     tail_v = tail[...]
     dx = dxl[...] + STEP_SIZE * tail_v * mm(b[...], carry_all)
     dbv = db[...] + STEP_SIZE * mm_t((tail_v * x[...].astype(F32)).astype(BF16), carry_all)
     dproj = jnp.concatenate([dx.astype(BF16), dbv.astype(BF16), dc[...].astype(BF16)], axis=1)
+    uv = u[...]
+    depth = uv.shape[1]
+    ready = 0
+    for j in range(dproj.shape[1] // LANES):
+        grads_out[ready:ready + depth, :] = t_mm(uv, dproj[:, cut(j)]).astype(BF16)
+        late.begin(ready, ready + depth)
+        ready += depth
     beside()
     du = mm_t(dproj, w_in[...]).astype(BF16)
     erv = er[...]
     width = erv.shape[1]
     for j in range(du.shape[1] // LANES):
-        grads_out[width * j:width * (j + 1), :] = t_mm(erv, du[:, cut(j)]).astype(BF16)
-    base = width * (du.shape[1] // LANES)
-    uv = u[...]
-    depth = uv.shape[1]
-    for j in range(dproj.shape[1] // LANES):
-        grads_out[base + depth * j:base + depth * (j + 1), :] = t_mm(uv, dproj[:, cut(j)]).astype(BF16)
+        grads_out[ready:ready + width, :] = t_mm(erv, du[:, cut(j)]).astype(BF16)
+        late.begin(ready, ready + width)
+        ready += width
     return du
 
 
-def unpack(gout, grads, arrived, grad_up, grad_in, grad_out, grad_skip, grad_table):
+def unpack(gout_in, grads_in, arrived_in, out_up, out_in, out_out, grad_skip, out_table,
+           gout, grads, arrived, grad_up, grad_in, grad_out, grad_table, in_sems, out_sems):
+    pairs = ((gout_in, gout), (grads_in, grads), (arrived_in, arrived))
+    ins = [pltpu.make_async_copy(src, dst, in_sems.at[n]) for n, (src, dst) in enumerate(pairs)]
+    pairs = ((grad_out, out_out), (grad_in, out_in), (grad_up, out_up), (grad_table, out_table))
+    outs = [pltpu.make_async_copy(src, dst, out_sems.at[n]) for n, (src, dst) in enumerate(pairs)]
+    for copy in ins:
+        copy.start()
     inner = grad_out.shape[0]
+    ins[0].wait()
     for j in range(grad_out.shape[1] // LANES):
         grad_out[:, cut(j)] = gout[inner * j:inner * (j + 1), :].astype(F32)
+    outs[0].start()
     width, depth = grad_up.shape
+    ins[1].wait()
+    for j in range(grad_in.shape[1] // LANES):
+        grad_in[:, cut(j)] = grads[depth * j:depth * (j + 1), :].astype(F32)
+    outs[1].start()
+    base = depth * (grad_in.shape[1] // LANES)
     for j in range(depth // LANES):
-        grad_up[:, cut(j)] = grads[width * j:width * (j + 1), :].astype(F32)
-    base = width * (depth // LANES)
-    for j in range(grad_in.shape[1] // LANES):
-        grad_in[:, cut(j)] = grads[base + depth * j:base + depth * (j + 1), :].astype(F32)
+        grad_up[:, cut(j)] = grads[base + width * j:base + width * (j + 1), :].astype(F32)
+    outs[2].start()
+    ins[2].wait()
     tags = arrived[:, width:].astype(F32)
     number = tags[:, 0:1] * 256.0 + tags[:, 1:2] - 1.0
     slots = tags.shape[0]
     row = lax.broadcasted_iota(jnp.int32, (slots, ROWS_DEV), 1).astype(F32)
     pick = jnp.where(row == number, 1.0, 0.0).astype(BF16)
     grad_table[...] = t_mm(pick, arrived[:, :width])
+    outs[3].start()
     heads = grad_skip.shape[1]
     cap = TILE
     parts = jnp.sum(tags.reshape(slots // cap, cap, LANES), axis=0)[:heads]
@@ -200,6 +218,8 @@
     same = lax.broadcasted_iota(jnp.int32, (heads, heads), 0) == lax.broadcasted_iota(
         jnp.int32, (heads, heads), 1)
     grad_skip[...] = jnp.sum(jnp.where(same, sums, 0.0), axis=0, keepdims=True)
+    for copy in outs:
+        copy.wait()
 
 
 def bit_count(n):
@@ -214,6 +234,7 @@
         self.levels = len(names) - 1
         tiles = rows // (batch_n * ctx_n) // TILE
         self.streams = []
+        self.ends = []
         base = 0
         recv = 0
         self.sems = 0
@@ -236,6 +257,7 @@
                 self.sems += 2 * others
             self.streams.append((base, plan))
             base += size
+            self.ends.append((base, size))
         self.recv_rows = recv
 
     def scratch(self, rows):
@@ -284,10 +306,11 @@
             self.copies.append((down, up))
             self.keeps.append(keeps)
 
-    def begin(self):
-        for down, _ in self.copies:
-            for copy in down[0]:
-                copy.start()
+    def begin(self, low, high):
+        for (end, _), (down, _) in zip(self.ends, self.copies):
+            if low < end <= high:
+                for copy in down[0]:
+                    copy.start()
 
     def step(self, k):
         last = self.levels - 1
@@ -371,7 +394,7 @@
     early.bind(where, e_acc, e_recv, e_full, e_send, e_got)
     late.bind(where, l_acc, l_recv, l_full, l_send, l_got)
     within(kept, hs, dout, skip, w_out.shape[0], dxl, db, dc, e_acc, y_buf, dsk)
-    early.begin()
+    early.begin(0, e_acc.shape[0])
     width = er.shape[1]
     pick, tags = route(cap, rows.shape[0], idx[...], dsk[...])
     pick_buf[...] = pick
@@ -432,9 +455,8 @@
         for hop in hops:
             hop.wait_send()
 
-    du = back(lambda: early.step(done), er, u, x, b, dxl, tail, db, dc, carry, w_in, l_acc)
+    du = back(late, lambda: early.step(done), er, u, x, b, dxl, tail, db, dc, carry, w_in, l_acc)
     done += 1
-    late.begin()
     rows[:, :width] = mm(pick_buf[...], mm_t(du, w_up[...]).astype(BF16)).astype(BF16)
     own_rows = pl.ds(pl.multiple_of(me * cap, TILE), cap)
     own = pltpu.make_async_copy(rows.at[own_rows], arrived.at[own_rows], own_sem)
@@ -544,8 +566,19 @@
             shape((width, depth), F32), shape((depth, proj), F32), shape((inner, depth), F32),
             shape((1, heads), F32), shape((ROWS_DEV, width), F32),
         ),
-        in_specs=[VMEM] * 3,
-        out_specs=[VMEM] * 5,
+        in_specs=[pl.BlockSpec(memory_space=pl.ANY)] * 3,
+        out_specs=[pl.BlockSpec(memory_space=pl.ANY)] * 3 + [VMEM, pl.BlockSpec(memory_space=pl.ANY)],
+        scratch_shapes=[
+            pltpu.VMEM(gout.shape, BF16),
+            pltpu.VMEM(grads.shape, BF16),
+            pltpu.VMEM(arrived.shape, BF16),
+            pltpu.VMEM((width, depth), F32),
+            pltpu.VMEM((depth, proj), F32),
+            pltpu.VMEM((inner, depth), F32),
+            pltpu.VMEM((ROWS_DEV, width), F32),
+            pltpu.SemaphoreType.DMA((3,)),
+            pltpu.SemaphoreType.DMA((4,)),
+        ],
         compiler_params=params,
         name="unpack",
     )(gout, grads, arrived)

time: 76.7 us -> 76.8 us (level)
  no operation moved by 1% of the time
where the time goes in v3:
time: 76.8 us; the launch traced here: 76.7 us
  Pallas kernels  76 us (99%)
    pallas_call x1, Pallas kernels, local(): pl.pallas_call(partial(middle, early, late, cap, batch_n, ctx_n), out_sha...  71.4 us
    pallas_call x1, Pallas kernels, local(): pl.pallas_call(unpack, out_shape=(shape((width, depth), F32), shape((dept...  4.58 us

profile of v3, /device:TPU:0, one launch (start us, length us, event | category | flops | bytes accessed | tf_op | source)
XLA Modules:
  0.0 76.7 jit_solution(12150308517697824576)
XLA Ops:
  0.6 71.4 %middle.1 = (bf16[4096,128]{1,0:T(8,128)(2,1)}, bf16[6144,128]{1,0:T(8,128)(2,1)}, bf16[512,384]{1,0:T(8,128)(2,1)}) custom-call(bf16[256,256]{1,0:T(8,128)(2,1)} %bitcast.11, s32[1,256]{1,0:T(1,128)} %idx.1, f32[16,256]{1,0:T(8,128)} %bitcast.12, f32[1024,128]{1,0:T(8,128)} %bitcast.9, bf16[256,512]{1,0:T(8,128)(2,1)} %bitcast.10, bf16[256,512]{1,0:T(8,128)(2,1)} %w_up.1, ...), custom_call_target="tpu_custom_call" | custom-call | tf_op jit(solution)/shard_map/middle/pallas_call | solution.py:521
  72.1 4.6 %unpack.1 = (f32[256,512]{1,0:T(8,128)}, f32[512,1280]{1,0:T(8,128)}, f32[1024,512]{1,0:T(8,128)}, f32[1,16]{1,0:T(1,128)}, f32[512,256]{1,0:T(8,128)}) custom-call(bf16[4096,128]{1,0:T(8,128)(2,1)} %get-tuple-element.13.gout_in, bf16[6144,128]{1,0:T(8,128)(2,1)} %get-tuple-element.14.grads_in, bf16[512,384]{1,0:T(8,128)(2,1)} %get-tuple-element.15.arrived_in), custom_call_target="tpu_custom_call" | custom-call | tf_op jit(solution)/shard_map/unpack/pallas_call | solution.py:563
